TPU v7x, 128 devices: a whole 4x4x4 slice. The times are simulated.
128 devices in a mesh: dp: 32 (over y, z, core), tensor: 4 (over x).
Axes of the slice: x: 4, y: 4, z: 4, core: 2. Of those that a mesh axis runs over, the one named last changes fastest.
Arguments:
- queries: bfloat16 [4096, 4096], P('dp', 'tensor'), may hold values from -120 to 120
- token_keys: bfloat16 [4096, 512], P('dp', 'tensor'), may hold values from -4 to 4
- token_values: bfloat16 [4096, 512], P('dp', 'tensor'), may hold values from -4 to 4
- cached_key_rows: bfloat16 [4096, 256, 512], P('dp', None, 'tensor'), may hold values from -4 to 4
- cached_value_rows: bfloat16 [4096, 256, 512], P('dp', None, 'tensor'), may hold values from -4 to 4
- cache_length: int32 [4096], P('dp'), may hold values from 2 to 256, as said below
- output_projection: bfloat16 [4096, 8192], P(None, 'tensor'), may hold values from -0.75 to 0.75
- request_adapter: int32 [4096], P('dp'), may hold values from 0 to 31, as said below
- adapter_table_row: int32 [32], replicated, may hold values from 0 to 31, each once
- adapter_down_weight: bfloat16 [32, 64, 4096], P('dp', None, 'tensor'), may hold values from -0.75 to 0.75
- adapter_up_weight: bfloat16 [32, 64, 8192], P('dp', None, 'tensor'), may hold values from -0.75 to 0.75
Outputs:
- mixed: bfloat16 [4096, 8192], P('dp', 'tensor')
Inputs may be any that keep to these rules, and one draw needn't show every extreme that they name: `cache_length`: at least one request has exactly 256 used positions. `request_adapter`: among the 128 requests of one index of dp no adapter id occurs more than 8 times; in every draw one adapter id occurs exactly 8 times on every index of dp. `adapter_table_row`: each row 0 to 31 is named once.
All inputs are finite; a program needn't handle non-finite values.
Results may differ from a plain program's by a relative error of at most 0.01.
Values may be sent and summed in bfloat16 or wider, within the bound.
No kernel may reach another device: no remote copies, remote signals or barrier semaphores. Data moves between devices by JAX's collectives and lax.ppermute only.
A program may use at most 128 MiB of HBM per device.

v0:
```python
import math
import jax
import jax.numpy as jnp
from jax import lax
from jax.sharding import PartitionSpec as P

HEADS = 32
KV_HEADS = 4
HEAD_DIM = 128


def attend(queries, token_keys, token_values, cached_key_rows, cached_value_rows, cache_length):
    requests = queries.shape[0]
    kv_local = token_keys.shape[1] // HEAD_DIM
    per_group = HEADS // KV_HEADS
    positions = cached_key_rows.shape[1]
    score_scale = 1.0 / math.sqrt(HEAD_DIM)
    query_heads = queries.reshape(requests, kv_local, per_group, HEAD_DIM)
    key_blocks = cached_key_rows.reshape(requests, positions, kv_local, HEAD_DIM)
    value_blocks = cached_value_rows.reshape(requests, positions, kv_local, HEAD_DIM)
    fresh_keys = token_keys.reshape(requests, kv_local, HEAD_DIM)
    fresh_values = token_values.reshape(requests, kv_local, HEAD_DIM)
    cached_score = (
        jnp.einsum("rkgd,rpkd->rkgp", query_heads, key_blocks, preferred_element_type=jnp.float32)
        * score_scale
    )
    fresh_score = (
        jnp.einsum("rkgd,rkd->rkg", query_heads, fresh_keys, preferred_element_type=jnp.float32)
        * score_scale
    )
    in_cache = (jnp.arange(positions, dtype=jnp.int32)[None, :] < cache_length[:, None])[
        :, None, None, :
    ]
    row_max = jnp.maximum(
        jnp.max(jnp.where(in_cache, cached_score, -jnp.inf), axis=-1), fresh_score
    )
    cached_weight = jnp.where(in_cache, jnp.exp(cached_score - row_max[..., None]), 0.0)
    fresh_weight = jnp.exp(fresh_score - row_max)
    weight_sum = jnp.sum(cached_weight, axis=-1) + fresh_weight
    combined = jnp.einsum(
        "rkgp,rpkd->rkgd",
        cached_weight.astype(jnp.bfloat16),
        value_blocks,
        preferred_element_type=jnp.float32,
    )
    combined = combined + jnp.einsum(
        "rkg,rkd->rkgd",
        fresh_weight.astype(jnp.bfloat16),
        fresh_values,
        preferred_element_type=jnp.float32,
    )
    return (
        (combined / weight_sum[..., None])
        .reshape(requests, kv_local * per_group * HEAD_DIM)
        .astype(jnp.bfloat16)
    )


def on_device(
    queries,
    token_keys,
    token_values,
    cached_key_rows,
    cached_value_rows,
    cache_length,
    output_projection,
    request_adapter,
    adapter_table_row,
    adapter_down_weight,
    adapter_up_weight,
):
    attention_output = attend(
        queries, token_keys, token_values, cached_key_rows, cached_value_rows, cache_length
    )
    requests = attention_output.shape[0]
    feature_cols = attention_output.shape[1]
    projected = jnp.dot(
        lax.all_gather(attention_output, "tensor", axis=1, tiled=True),
        output_projection,
        preferred_element_type=jnp.float32,
    )
    every_adapter = adapter_table_row.shape[0]
    table_capacity = 2 * requests // every_adapter
    matches = request_adapter[:, None] == jnp.arange(every_adapter, dtype=jnp.int32)[None, :]
    slot_of = jnp.sum(jnp.where(matches, adapter_table_row[None, :], 0), axis=1)
    request_order = jnp.arange(requests, dtype=jnp.int32)
    earlier = (slot_of[:, None] == slot_of[None, :]) & (
        request_order[:, None] > request_order[None, :]
    )
    position = slot_of * table_capacity + jnp.sum(earlier.astype(jnp.int32), axis=1)
    placing = (
        jnp.arange(every_adapter * table_capacity, dtype=jnp.int32)[:, None] == position[None, :]
    ).astype(jnp.bfloat16)
    buffer_rows = jnp.dot(placing, attention_output, preferred_element_type=jnp.float32).astype(
        jnp.bfloat16
    )
    table_down, table_up = (
        lax.all_gather(adapter_down_weight, "dp", axis=0, tiled=True),
        lax.all_gather(adapter_up_weight, "dp", axis=0, tiled=True),
    )
    grouped = buffer_rows.reshape(every_adapter, table_capacity, feature_cols)
    rank_terms = jnp.einsum("acw,arw->acr", grouped, table_down, preferred_element_type=jnp.float32)
    low_rank_state = lax.psum(rank_terms, "tensor").astype(jnp.bfloat16)
    adapter_deltas = jnp.einsum(
        "acr,ard->acd", low_rank_state, table_up, preferred_element_type=jnp.float32
    ).astype(jnp.bfloat16)
    adapter_deltas = adapter_deltas.reshape(
        every_adapter * table_capacity, adapter_up_weight.shape[2]
    )
    returned = jnp.einsum("sr,sd->rd", placing, adapter_deltas, preferred_element_type=jnp.float32)
    return (projected + returned).astype(jnp.bfloat16)


def solution(mesh):
    in_specs = (
        P("dp", "tensor"),
        P("dp", "tensor"),
        P("dp", "tensor"),
        P("dp", None, "tensor"),
        P("dp", None, "tensor"),
        P("dp"),
        P(None, "tensor"),
        P("dp"),
        P(),
        P("dp", None, "tensor"),
        P("dp", None, "tensor"),
    )
    out_specs = P("dp", "tensor")
    return jax.shard_map(
        on_device, mesh=mesh, in_specs=in_specs, out_specs=out_specs, check_vma=False
    )
```

profile of v0, /device:TPU:1, one launch (start us, length us, event | category | flops | bytes accessed | tf_op | source)
XLA Modules:
  0.0 161.0 jit_solution(15225295024856014704)
XLA Ops:
  6.5 0.0 copy-start
  6.5 0.0 copy-start.1
  6.5 0.0 all-gather.4.cloned.1.call-start
  6.5 0.0 copy-start.2
  6.5 0.9 iota_compare_fusion.4
  7.4 1.4 copy.14
  8.9 0.0 copy-done
  8.9 0.3 fusion.17
  9.1 5.7 %select_reduce_fusion = (f32[128,8]{1,0:T(8,128)S(1)}, f32[128,8,256]{2,1,0:T(8,128)S(1)}) fusion(pred[128,256]{1,0:T(8,128)(4,1)S(1)} %iota_compare_fusion.4, bf16[128,8,128]{2,1,0:T(8,128)(2,1)S(1)} %bitcast.32, bf16[128,256,128]{2,1,0:T(8,128)(2,1)} %param.14), kind=kOutput, calls=%fused_computation.11 | convolution fusion | flops 67894272 | bytes 9736192 | tf_op jit(solution)/shard_map/rkgd,rpkd->rkgp/dot_general | solution.py:24
  14.9 0.0 copy-start.3
  14.9 0.0 copy-start.4
  14.9 0.4 fusion.5
  15.3 0.0 copy-done.1
  15.4 0.0 copy-done.2
  15.4 1.3 fusion.4
  16.7 0.8 copy.21
  17.4 0.0 all-gather.4.cloned.1.call-update
  17.5 0.0 all-gather.6.cloned.1.call-start
  17.5 0.7 all-gather.6.cloned.1.call-update
  18.2 0.0 all-gather.8.cloned.1.call-start
  18.3 0.7 all-gather.8.cloned.1.call-update
  18.9 0.0 copy-done.3
  19.0 0.0 copy-done.4
  19.0 0.1 select_reduce_fusion.1
  19.1 0.2 convert_reduce_fusion
  19.2 24.6 %all-gather.4.cloned.1.call-done = bf16[128,4096]{1,0:T(8,128)(2,1)} async-done(((bf16[128,1024]{1,0:T(8,128)(2,1)}), bf16[128,4096]{1,0:T(8,128)(2,1)}) %all-gather.4.cloned.1.call-update) | async-done | bytes 1048592 | tf_op jit(solution)/shard_map/all_gather | solution.py:78
  43.9 8.4 %fusion.22 = f32[128,2048]{1,0:T(8,128)S(1)} fusion(bf16[128,4096]{1,0:T(8,128)(2,1)} %all-gather.4.cloned.1.call-done, bf16[4096,2048]{1,0:T(8,128)(2,1)} %param.17), kind=kOutput, calls=%fused_computation.37 | convolution fusion | flops 2147483648 | bytes 18874368 | tf_op jit(solution)/shard_map/dot_general | solution.py:77
  52.3 41.9 %all-gather.6.cloned.1.call-done = bf16[32,64,1024]{2,1,0:T(8,128)(2,1)} async-done(((bf16[1,64,1024]{2,1,0:T(8,128)(2,1)}), bf16[32,64,1024]{2,1,0:T(8,128)(2,1)}) %all-gather.6.cloned.1.call-update) | async-done | bytes 4194320 | tf_op jit(solution)/shard_map/all_gather | solution.py:98
  94.2 3.5 %fusion.7 = f32[32,8,64]{2,1,0:T(8,128)S(1)} fusion(bf16[32,64,1024]{2,1,0:T(8,128)(2,1)} %all-gather.6.cloned.1.call-done, s32[128]{0:T(128)S(1)} %multiply_add_fusion, bf16[16,8,8,128]{3,2,1,0:T(8,128)(2,1)S(1)} %bitcast.30), kind=kOutput, calls=%fused_computation.14 | convolution fusion | flops 100958208 | bytes 4522496 | tf_op jit(solution)/shard_map/acw,arw->acr/dot_general | solution.py:102
  97.8 14.6 %psum.7 = bf16[32,8,64]{2,1,0:T(8,128)(2,1)S(1)} all-reduce(f32[32,8,64]{2,1,0:T(8,128)S(1)} %fusion.7), channel_id=1, replica_groups=mesh['dp'=32,'tensor'=4] {'tensor'}, use_global_device_ids=true, to_apply=%region_4.5 | all-reduce | flops 16384 | bytes 98304 | tf_op jit(solution)/shard_map/psum | solution.py:103
  112.3 36.5 %all-gather.8.cloned.1.call-done = bf16[32,64,2048]{2,1,0:T(8,128)(2,1)} async-done(((bf16[1,64,2048]{2,1,0:T(8,128)(2,1)}), bf16[32,64,2048]{2,1,0:T(8,128)(2,1)}) %all-gather.8.cloned.1.call-update) | async-done | bytes 8388624 | tf_op jit(solution)/shard_map/all_gather | solution.py:99
  148.8 5.6 %fusion.1 = bf16[128,2048]{1,0:T(8,128)(2,1)} fusion(f32[128,2048]{1,0:T(8,128)S(1)} %fusion.22, bf16[32,64,2048]{2,1,0:T(8,128)(2,1)} %all-gather.8.cloned.1.call-done, bf16[32,8,64]{2,1,0:T(8,128)(2,1)S(1)} %psum.7, s32[128]{0:T(128)S(1)} %multiply_add_fusion), kind=kOutput, calls=%fused_computation.3 | convolution fusion | flops 202407936 | bytes 9994752 | tf_op jit(solution)/shard_map/sr,sd->rd/dot_general | solution.py:110
  (4 shorter events, 0.1 us)
Async XLA Ops:
  6.5 2.3 %copy-start = (bf16[128,128]{1,0:T(8,128)(2,1)S(1)}, bf16[128,128]{1,0:T(8,128)(2,1)}, u32[]{:S(2)}) copy-start(bf16[128,128]{1,0:T(8,128)(2,1)} %param.12) | copy-start | bytes 98308
  6.5 8.8 %copy-start.1 = (bf16[128,128]{1,0:T(8,128)(2,1)S(1)}, bf16[128,128]{1,0:T(8,128)(2,1)}, u32[]{:S(2)}) copy-start(bf16[128,128]{1,0:T(8,128)(2,1)} %param.13) | copy-start | bytes 98308
  6.5 37.3 %all-gather.4.cloned.1.call-start = ((), (), s32[]{:S(2)}) async-start(), calls=%async_computation | async-start | bytes 1310720 | tf_op jit(solution)/shard_map/all_gather | solution.py:78
  6.5 8.8 %copy-start.2 = (bf16[128,256,128]{2,1,0:T(8,128)(2,1)S(1)}, bf16[128,256,128]{2,1,0:T(8,128)(2,1)}, u32[]{:S(2)}) copy-start(bf16[128,256,128]{2,1,0:T(8,128)(2,1)} %param.15) | copy-start | bytes 25165828
  14.9 4.1 %copy-start.3 = (s32[32]{0:T(128)S(1)}, s32[32]{0:T(128)}, u32[]{:S(2)}) copy-start(s32[32]{0:T(128)} %param.19) | copy-start | bytes 388
  14.9 4.1 %copy-start.4 = (s32[128]{0:T(128)S(1)}, s32[128]{0:T(128)}, u32[]{:S(2)}) copy-start(s32[128]{0:T(128)} %param.18) | copy-start | bytes 1540
  17.5 76.8 %all-gather.6.cloned.1.call-start = ((), (), s32[]{:S(2)}) async-start(), calls=%async_computation.1 | async-start | bytes 4325376 | tf_op jit(solution)/shard_map/all_gather | solution.py:98
  18.2 130.6 %all-gather.8.cloned.1.call-start = ((), (), s32[]{:S(2)}) async-start(), calls=%async_computation.2 | async-start | bytes 8650752 | tf_op jit(solution)/shard_map/all_gather | solution.py:99
Sparse Core Ops, SparseCore 0:
  17.6 26.2 all-gather.3
  46.1 48.0 all-gather.5
  96.5 52.2 all-gather.7
where the time goes:
time: 161 us
  waiting for transfers between devices  104 us (65%)
  matrix products  24.9 us (15%)
  blocking collectives  14.6 us (9%)
  between operations  13.2 us (8%)
  local copies, waits for them, and re-layouts  2.18 us (1%)
    all_gather x1, waiting for transfers between devices, on_device(): lax.all_gather(adapter_down_weight, 'dp', axis=0, tiled=True)  41.9 us
    all_gather x1, waiting for transfers between devices, on_device(): lax.all_gather(adapter_up_weight, 'dp', axis=0, tiled=True)  36.5 us
    all_gather x1, waiting for transfers between devices, on_device(): lax.all_gather(attention_output, 'tensor', axis=1, tiled=True)  24.6 us
    psum x1, blocking collectives, on_device(): low_rank_state = lax.psum(rank_terms, 'tensor').astype(jnp.bfloat16)  14.6 us
    dot_general x1, matrix products, on_device(): jnp.dot(lax.all_gather(attention_output, 'tensor', axis=1, tiled=True), o...  8.43 us
    dot_general x1, matrix products, attend(): jnp.einsum('rkgd,rpkd->rkgp', query_heads, key_blocks, preferred_element_...  5.74 us
    dot_general x1, matrix products, on_device(): jnp.einsum('sr,sd->rd', placing, adapter_deltas, preferred_element_type=j...  5.62 us
    dot_general x1, matrix products, on_device(): jnp.einsum('acw,arw->acr', grouped, table_down, preferred_element_type=jn...  3.54 us
  transfers between devices with their start and end apart: 3, of which 3 were waited for; matrix products, arithmetic and copies ran while one was open for 8% of the time, Pallas kernels for 0%

commit v1 on v0

--- a/solution.py
+++ b/solution.py
@@ -3,6 +3,7 @@
 import jax.numpy as jnp
 from jax import lax
 from jax.sharding import PartitionSpec as P
+from jax.lax import all_to_all, axis_size
 
 HEADS = 32
 KV_HEADS = 4
@@ -69,15 +70,22 @@
     adapter_down_weight,
     adapter_up_weight,
 ):
+
+    def switch_values(piece_in):
+        return jnp.concatenate(
+            all_to_all(
+                jnp.stack([piece_in for _ in range(axis_size("tensor"))], 0), "tensor", 0, 0
+            ),
+            axis=1,
+        )
+
     attention_output = attend(
         queries, token_keys, token_values, cached_key_rows, cached_value_rows, cache_length
     )
     requests = attention_output.shape[0]
     feature_cols = attention_output.shape[1]
     projected = jnp.dot(
-        lax.all_gather(attention_output, "tensor", axis=1, tiled=True),
-        output_projection,
-        preferred_element_type=jnp.float32,
+        switch_values(attention_output), output_projection, preferred_element_type=jnp.float32
     )
     every_adapter = adapter_table_row.shape[0]
     table_capacity = 2 * requests // every_adapter

time: 161 us -> 127 us (0.79)
  waiting for transfers between devices: 104 us -> 63.5 us
  starting transfers between devices: 0.08 us -> 4.88 us
    all_gather x1, waiting for transfers between devices: 41.9 us -> 11.8 us  [on_device(): lax.all_gather(adapter_down_weight, 'dp', axis=0, tiled=True)]
    all_gather x1 -> x0, waiting for transfers between devices: 24.6 us -> none  [on_device(): lax.all_gather(attention_output, 'tensor', axis=1, tiled=True)]
    all_to_all x0 -> x1, waiting for transfers between devices: none -> 13.9 us  [switch_values(): all_to_all(jnp.stack([piece_in for _ in range(axis_size('tensor'))], 0),...]
    all_to_all x0 -> x1, starting transfers between devices: none -> 4.84 us  [switch_values(): all_to_all(jnp.stack([piece_in for _ in range(axis_size('tensor'))], 0),...]
  transfers between devices with their start and end apart: 3 -> 3, of which waited for: 3 -> 3; matrix products, arithmetic and copies ran while one was open for 8% -> 19% of each run, Pallas kernels for 0% -> 0%
where the time goes in v1:
time: 127 us
  waiting for transfers between devices  63.5 us (50%)
  matrix products  24.9 us (20%)
  blocking collectives  14.6 us (11%)
  between operations  13.5 us (11%)
  starting transfers between devices  4.88 us (4%)
  other arithmetic  2.75 us (2%)
  local copies, waits for them, and re-layouts  2.57 us (2%)
    all_gather x1, waiting for transfers between devices, on_device(): lax.all_gather(adapter_up_weight, 'dp', axis=0, tiled=True)  36.5 us
    psum x1, blocking collectives, on_device(): low_rank_state = lax.psum(rank_terms, 'tensor').astype(jnp.bfloat16)  14.6 us
    all_to_all x1, waiting for transfers between devices, switch_values(): all_to_all(jnp.stack([piece_in for _ in range(axis_size('tensor'))], 0),...  13.9 us
    all_gather x1, waiting for transfers between devices, on_device(): lax.all_gather(adapter_down_weight, 'dp', axis=0, tiled=True)  11.8 us
    dot_general x1, matrix products, on_device(): jnp.dot(switch_values(attention_output), output_projection, preferred_ele...  8.47 us
    dot_general x1, matrix products, attend(): jnp.einsum('rkgd,rpkd->rkgp', query_heads, key_blocks, preferred_element_...  5.74 us
    dot_general x1, matrix products, on_device(): jnp.einsum('sr,sd->rd', placing, adapter_deltas, preferred_element_type=j...  5.62 us
    all_to_all x1, starting transfers between devices, switch_values(): all_to_all(jnp.stack([piece_in for _ in range(axis_size('tensor'))], 0),...  4.84 us
  transfers between devices with their start and end apart: 3, of which 3 were waited for; matrix products, arithmetic and copies ran while one was open for 19% of the time, Pallas kernels for 0%

profile of v1, /device:TPU:1, one launch (start us, length us, event | category | flops | bytes accessed | tf_op | source)
XLA Modules:
  0.0 126.8 jit_solution(2980121256509311594)
XLA Ops:
  6.5 0.0 copy-start
  6.5 0.0 all-gather.3.cloned.1.call-start
  6.5 0.7 all-gather.3.cloned.1.call-update
  7.3 0.0 all-gather.5.cloned.1.call-start
  7.3 0.7 all-gather.5.cloned.1.call-update
  8.0 0.0 copy-start.1
  8.0 1.1 copy.17
  9.2 1.0 convert.7
  10.2 1.0 iota_compare_fusion.4
  11.2 0.0 copy-done
  11.2 0.3 fusion.17
  11.5 5.7 %select_reduce_fusion = (f32[128,8]{1,0:T(8,128)S(1)}, f32[128,8,256]{2,1,0:T(8,128)S(1)}) fusion(pred[128,256]{1,0:T(8,128)(4,1)S(1)} %iota_compare_fusion.4, bf16[128,8,128]{2,1,0:T(8,128)(2,1)S(1)} %bitcast.36, bf16[128,256,128]{2,1,0:T(8,128)(2,1)} %param.14), kind=kOutput, calls=%fused_computation.11 | convolution fusion | flops 67894272 | bytes 9736192 | tf_op jit(solution)/shard_map/rkgd,rpkd->rkgp/dot_general | solution.py:25
  17.2 0.0 copy-start.2
  17.2 0.0 copy-start.3
  17.3 0.4 fusion.5
  17.7 0.0 copy-done.1
  17.7 1.3 %fusion.4 = bf16[128,8,128]{2,1,0:T(8,128)(2,1)S(1)} fusion(bf16[128,256,128]{2,1,0:T(8,128)(2,1)S(1)} %copy-done.1, f32[128,8,256]{2,1,0:T(8,128)S(1)} %get-tuple-element.8, f32[128,8]{1,0:T(8,128)S(1)} %multiply_maximum_fusion, pred[128,256]{1,0:T(8,128)(4,1)S(1)} %iota_compare_fusion.4, f32[128,8]{1,0:T(8,128)S(1)} %get-tuple-element.6, ...), kind=kOutput, calls=%fused_computation.9 | convolution fusion | flops 68419584 | bytes 9809920 | tf_op jit(solution)/shard_map/rkgp,rpkd->rkgd/dot_general | solution.py:41
  19.0 0.1 copy.24
  19.1 0.2 copy.14
  19.3 1.2 stack.2
  20.4 4.8 %all-to-all-start = ((bf16[4,128,1024]{1,2,0:T(8,128)(2,1)}), bf16[4,128,1024]{1,2,0:T(8,128)(2,1)S(1)}, u32[]{:S(2)}, u32[]{:S(2)}) async-start(bf16[4,128,1024]{1,2,0:T(8,128)(2,1)} %stack.2), calls=%async_computation | async-start | bytes 2097152 | tf_op jit(solution)/shard_map/all_to_all | solution.py:76
  25.3 0.0 copy-done.2
  25.3 0.0 copy-done.3
  25.3 0.1 select_reduce_fusion.1
  25.4 0.2 convert_reduce_fusion
  25.6 13.9 %all-to-all-done = bf16[4,128,1024]{1,2,0:T(8,128)(2,1)S(1)} async-done(((bf16[4,128,1024]{1,2,0:T(8,128)(2,1)}), bf16[4,128,1024]{1,2,0:T(8,128)(2,1)S(1)}, u32[]{:S(2)}, u32[]{:S(2)}) %all-to-all-start) | async-done | bytes 1048608 | tf_op jit(solution)/shard_map/all_to_all | solution.py:76
  39.5 8.5 %fusion.22 = f32[128,2048]{1,0:T(8,128)S(1)} fusion(bf16[128,4096]{0,1:T(8,128)(2,1)S(1)} %bitcast.32, bf16[4096,2048]{1,0:T(8,128)(2,1)} %param.17), kind=kOutput, calls=%fused_computation.37 | convolution fusion | flops 2147483648 | bytes 18874368 | tf_op jit(solution)/shard_map/dot_general | solution.py:87
  47.9 11.8 %all-gather.3.cloned.1.call-done = bf16[32,64,1024]{2,1,0:T(8,128)(2,1)} async-done(((bf16[1,64,1024]{2,1,0:T(8,128)(2,1)}), bf16[32,64,1024]{2,1,0:T(8,128)(2,1)}) %all-gather.3.cloned.1.call-update) | async-done | bytes 4194320 | tf_op jit(solution)/shard_map/all_gather | solution.py:106
  59.7 3.5 %fusion.7 = f32[32,8,64]{2,1,0:T(8,128)S(1)} fusion(bf16[32,64,1024]{2,1,0:T(8,128)(2,1)} %all-gather.3.cloned.1.call-done, s32[128]{0:T(128)S(1)} %multiply_add_fusion, bf16[16,8,8,128]{3,2,1,0:T(8,128)(2,1)S(1)} %bitcast.34), kind=kOutput, calls=%fused_computation.14 | convolution fusion | flops 100958208 | bytes 4522496 | tf_op jit(solution)/shard_map/acw,arw->acr/dot_general | solution.py:110
  63.2 14.6 %psum.7 = bf16[32,8,64]{2,1,0:T(8,128)(2,1)S(1)} all-reduce(f32[32,8,64]{2,1,0:T(8,128)S(1)} %fusion.7), channel_id=1, replica_groups=mesh['dp'=32,'tensor'=4] {'tensor'}, use_global_device_ids=true, to_apply=%region_4.5 | all-reduce | flops 16384 | bytes 98304 | tf_op jit(solution)/shard_map/psum | solution.py:111
  77.8 36.5 %all-gather.5.cloned.1.call-done = bf16[32,64,2048]{2,1,0:T(8,128)(2,1)} async-done(((bf16[1,64,2048]{2,1,0:T(8,128)(2,1)}), bf16[32,64,2048]{2,1,0:T(8,128)(2,1)}) %all-gather.5.cloned.1.call-update) | async-done | bytes 8388624 | tf_op jit(solution)/shard_map/all_gather | solution.py:107
  114.3 5.6 %fusion.1 = bf16[128,2048]{1,0:T(8,128)(2,1)} fusion(f32[128,2048]{1,0:T(8,128)S(1)} %fusion.22, bf16[32,64,2048]{2,1,0:T(8,128)(2,1)} %all-gather.5.cloned.1.call-done, bf16[32,8,64]{2,1,0:T(8,128)(2,1)S(1)} %psum.7, s32[128]{0:T(128)S(1)} %multiply_add_fusion), kind=kOutput, calls=%fused_computation.3 | convolution fusion | flops 202407936 | bytes 9994752 | tf_op jit(solution)/shard_map/sr,sd->rd/dot_general | solution.py:118
  (3 shorter events, 0.1 us)
Async XLA Ops:
  6.5 4.7 %copy-start = (bf16[128,128]{1,0:T(8,128)(2,1)S(1)}, bf16[128,128]{1,0:T(8,128)(2,1)}, u32[]{:S(2)}) copy-start(bf16[128,128]{1,0:T(8,128)(2,1)} %param.12) | copy-start | bytes 98308
  6.5 53.2 %all-gather.3.cloned.1.call-start = ((), (), s32[]{:S(2)}) async-start(), calls=%async_computation.1 | async-start | bytes 4325376 | tf_op jit(solution)/shard_map/all_gather | solution.py:106
  7.3 107.0 %all-gather.5.cloned.1.call-start = ((), (), s32[]{:S(2)}) async-start(), calls=%async_computation.2 | async-start | bytes 8650752 | tf_op jit(solution)/shard_map/all_gather | solution.py:107
  8.0 9.7 %copy-start.1 = (bf16[128,256,128]{2,1,0:T(8,128)(2,1)S(1)}, bf16[128,256,128]{2,1,0:T(8,128)(2,1)}, u32[]{:S(2)}) copy-start(bf16[128,256,128]{2,1,0:T(8,128)(2,1)} %param.15) | copy-start | bytes 25165828
  17.2 8.0 %copy-start.2 = (s32[32]{0:T(128)S(1)}, s32[32]{0:T(128)}, u32[]{:S(2)}) copy-start(s32[32]{0:T(128)} %param.19) | copy-start | bytes 388
  17.2 8.1 %copy-start.3 = (s32[128]{0:T(128)S(1)}, s32[128]{0:T(128)}, u32[]{:S(2)}) copy-start(s32[128]{0:T(128)} %param.18) | copy-start | bytes 1540
  20.4 19.0 %all-to-all-start = ((bf16[4,128,1024]{1,2,0:T(8,128)(2,1)}), bf16[4,128,1024]{1,2,0:T(8,128)(2,1)S(1)}, u32[]{:S(2)}, u32[]{:S(2)}) async-start(bf16[4,128,1024]{1,2,0:T(8,128)(2,1)} %stack.2), calls=%async_computation | async-start | bytes 2097152 | tf_op jit(solution)/shard_map/all_to_all | solution.py:76
Sparse Core Ops, SparseCore 0:
  9.6 50.0 all-gather.2
  62.0 52.2 all-gather.4
